TPU v7x, 32 devices: a whole 2x2x4 slice. The times are simulated.
32 devices in a mesh: dp: 8 (over z, x), fsdp: 4 (over y, core).
Axes of the slice: x: 2, y: 2, z: 4, core: 2. Of those that a mesh axis runs over, the one named last changes fastest.
Arguments:
- tokens: bfloat16 [32, 1024, 768], P(('dp', 'fsdp')), may hold values from -11 to 11
- lengths: int32 [32], P(('dp', 'fsdp')), may hold values from 256 to 1024, as said below
- buckets: int32 [2047], replicated, may hold values from 0 to 31
- rel_table: float32 [32, 12], replicated, may hold values from -4 to 4
- gain_attn: float32 [768], replicated, may hold values from 0.5 to 1.5
- gain_ff: float32 [768], replicated, may hold values from 0.5 to 1.5
- w_qkv: bfloat16 [768, 2304], replicated, may hold values from -0.21875 to 0.21875
- w_out: bfloat16 [768, 768], replicated, may hold values from -0.875 to 0.875
- w_in: bfloat16 [768, 3072], replicated, may hold values from -0.21875 to 0.21875
- w_down: bfloat16 [3072, 768], replicated, may hold values from -0.109375 to 0.109375
- adapters: bfloat16 [622080], P(('dp', 'fsdp')), may hold values from -5 to 5
- cotangent: bfloat16 [32, 1024, 768], P(('dp', 'fsdp')), may hold values from -6 to 6
Outputs:
- block_out: bfloat16 [32, 1024, 768], P(('dp', 'fsdp'))
- tokens_grad: float32 [32, 1024, 768], P(('dp', 'fsdp'))
- adapters_grad: float32 [622080], P(('dp', 'fsdp'))
- root_squares: float32 [4], replicated
Inputs may be any that keep to these rules, and one draw needn't show every extreme that they name: `lengths`: each sequence's count of valid leading positions; in every draw one sequence has all 1024.
All inputs are finite; a program needn't handle non-finite values.
Results may differ from a plain program's by a relative error of at most 0.017.
Values may be sent and summed in bfloat16 or wider, within the bound.
A program may use at most 512 MiB of HBM per device.

v0:
```python
import jax
import jax.numpy as jnp
from jax import lax
from jax.sharding import PartitionSpec as P

D = 768
FF = 3072
HEADS = 12
HDIM = 64
EXPERTS = 10
RANK = 4


EPSILON = 1e-06
MASKED = -1000000000.0
GELU_SCALE = 0.7978845608028654
GELU_CUBIC = 0.044715


def gelu_smooth(values):
    return (
        0.5
        * values
        * (1.0 + jnp.tanh(GELU_SCALE * (values + GELU_CUBIC * values * values * values)))
    )


def gelu_slope(values):
    tangent = jnp.tanh(GELU_SCALE * (values + GELU_CUBIC * values * values * values))
    return 0.5 * (1.0 + tangent) + 0.5 * values * (1.0 - tangent * tangent) * GELU_SCALE * (
        1.0 + 3.0 * GELU_CUBIC * values * values
    )


def unpack_adapters(flat_values):
    result = []
    offset = 0
    for fan_in, fan_out in ((D, D), (D, D), (D, D), (D, D), (D, FF), (FF, D)):
        layout = (
            ((fan_in, EXPERTS * RANK), fan_in * EXPERTS * RANK),
            ((EXPERTS * RANK, fan_out), EXPERTS * RANK * fan_out),
            ((fan_in, EXPERTS), fan_in * EXPERTS),
        )
        members = []
        for form_of, count_of in layout:
            members.append(flat_values[offset : offset + count_of].reshape(form_of))
            offset += count_of
        result.append(tuple(members))
    return result


def rms_forward(inputs, gain):
    inv_rms = lax.rsqrt(jnp.mean(inputs * inputs, axis=-1, keepdims=True) + EPSILON)
    return (inputs * inv_rms * gain, inv_rms)


def rms_backward(inputs, gain, inv_rms, grad_normed):
    weighted = grad_normed * gain
    return inv_rms * weighted - inputs * (inv_rms * inv_rms * inv_rms) * jnp.mean(
        inputs * weighted, axis=-1, keepdims=True
    )


def adapter_forward(inputs, adapter):
    down_proj, up_proj, router = adapter
    logits = jnp.dot(inputs, router, preferred_element_type=jnp.float32)
    gate_probs = jax.nn.softmax(logits, axis=-1)
    lowrank = jnp.dot(inputs, down_proj, preferred_element_type=jnp.float32)
    mixed_rank = (lowrank * jnp.repeat(gate_probs, RANK, axis=1)).astype(jnp.bfloat16)
    extra = jnp.dot(mixed_rank, up_proj, preferred_element_type=jnp.float32)
    return (extra, (gate_probs, lowrank, mixed_rank))


def adapter_backward(inputs, adapter, stored, grad_out):
    down_proj, up_proj, router = adapter
    gate_probs, lowrank, mixed_rank = stored
    grad_up = jnp.dot(mixed_rank.T, grad_out, preferred_element_type=jnp.float32)
    grad_mixed = jnp.dot(grad_out, up_proj.T, preferred_element_type=jnp.float32)
    grad_rank = (grad_mixed * jnp.repeat(gate_probs, RANK, axis=1)).astype(jnp.bfloat16)
    grad_gates = jnp.sum((grad_mixed * lowrank).reshape(-1, EXPERTS, RANK), axis=2)
    grad_logits = (
        gate_probs * (grad_gates - jnp.sum(gate_probs * grad_gates, axis=1, keepdims=True))
    ).astype(jnp.bfloat16)
    grad_in = jnp.dot(grad_rank, down_proj.T, preferred_element_type=jnp.float32)
    grad_in = grad_in + jnp.dot(grad_logits, router.T, preferred_element_type=jnp.float32)
    grad_down = jnp.dot(inputs.T, grad_rank, preferred_element_type=jnp.float32)
    grad_router = jnp.dot(inputs.T, grad_logits, preferred_element_type=jnp.float32)
    return (grad_in, (grad_down, grad_up, grad_router))


def block_bias(offset_bias, length, row_start, block_rows, seq_len):
    offsets = (
        jnp.arange(seq_len)[None, :] - jnp.arange(block_rows)[:, None] - row_start + (seq_len - 1)
    )
    gathered = jnp.take(offset_bias, offsets, axis=1)
    valid_keys = (jnp.arange(seq_len) < length)[None, None, :]
    return (gathered, valid_keys)


def attend_sequence(queries, key_heads, value_heads, length, offset_bias):
    seq_len = queries.shape[0]
    block_rows = min(512, seq_len)
    outputs = []
    log_totals = []
    for row_start in range(0, seq_len, block_rows):
        query_rows = queries[row_start : row_start + block_rows]
        bias_rows, valid_keys = block_bias(offset_bias, length, row_start, block_rows, seq_len)
        raw_scores = jnp.einsum(
            "qhd,khd->hqk", query_rows, key_heads, preferred_element_type=jnp.float32
        )
        scores = jnp.where(valid_keys, raw_scores * 0.125 + bias_rows, MASKED)
        row_peak = jnp.max(scores, axis=-1, keepdims=True)
        exp_scores = jnp.exp(scores - row_peak)
        row_total = jnp.sum(exp_scores, axis=-1, keepdims=True)
        weights_low = (exp_scores / row_total).astype(jnp.bfloat16)
        attended = jnp.einsum(
            "hqk,khd->qhd", weights_low, value_heads, preferred_element_type=jnp.float32
        )
        outputs.append(attended.astype(jnp.bfloat16))
        log_totals.append(row_peak + jnp.log(row_total))
    return (jnp.concatenate(outputs, axis=0), jnp.concatenate(log_totals, axis=1))


def attend_backward(
    queries, key_heads, value_heads, length, offset_bias, log_totals, grad_attended
):
    seq_len = queries.shape[0]
    block_rows = min(512, seq_len)
    grad_keys = jnp.zeros(key_heads.shape, jnp.float32)
    grad_values = jnp.zeros(value_heads.shape, jnp.float32)
    grad_queries = []
    for row_start in range(0, seq_len, block_rows):
        query_rows = queries[row_start : row_start + block_rows]
        grad_rows = grad_attended[row_start : row_start + block_rows]
        bias_rows, valid_keys = block_bias(offset_bias, length, row_start, block_rows, seq_len)
        raw_scores = jnp.einsum(
            "qhd,khd->hqk", query_rows, key_heads, preferred_element_type=jnp.float32
        )
        scores = jnp.where(valid_keys, raw_scores * 0.125 + bias_rows, MASKED)
        prob_rows = jnp.exp(scores - log_totals[:, row_start : row_start + block_rows])
        grad_values = grad_values + jnp.einsum(
            "hqk,qhd->khd",
            prob_rows.astype(jnp.bfloat16),
            grad_rows,
            preferred_element_type=jnp.float32,
        )
        grad_probs = jnp.einsum(
            "qhd,khd->hqk", grad_rows, value_heads, preferred_element_type=jnp.float32
        )
        row_delta = jnp.sum(prob_rows * grad_probs, axis=-1, keepdims=True)
        grad_raw = (prob_rows * (grad_probs - row_delta) * 0.125).astype(jnp.bfloat16)
        grad_queries.append(
            jnp.einsum(
                "hqk,khd->qhd", grad_raw, key_heads, preferred_element_type=jnp.float32
            ).astype(jnp.bfloat16)
        )
        grad_keys = grad_keys + jnp.einsum(
            "hqk,qhd->khd", grad_raw, query_rows, preferred_element_type=jnp.float32
        )
    return (
        jnp.concatenate(grad_queries, axis=0),
        grad_keys.astype(jnp.bfloat16),
        grad_values.astype(jnp.bfloat16),
    )


def per_device(
    tokens,
    lengths,
    buckets,
    rel_table,
    gain_attn,
    gain_ff,
    w_qkv,
    w_out,
    w_in,
    w_down,
    adapters,
    cotangent,
):
    seq_count, seq_len, width = tokens.shape
    pieces = unpack_adapters(lax.all_gather(adapters, ("dp", "fsdp"), axis=0, tiled=True))
    bucket_hits = (jnp.arange(rel_table.shape[0])[:, None] == buckets[None, :]).astype(jnp.float32)
    offset_bias = jnp.dot(rel_table.T, bucket_hits, precision=lax.Precision.HIGHEST)
    inputs = tokens.reshape(-1, width).astype(jnp.float32)
    normed_full, inv_attn = rms_forward(inputs, gain_attn)
    normed = normed_full.astype(jnp.bfloat16)
    dense_qkv = jnp.dot(normed, w_qkv, preferred_element_type=jnp.float32)
    heads_shape = (seq_count, seq_len, HEADS, HDIM)
    projected = []
    stored_qkv = []
    for proj_index in range(3):
        extra, stored = adapter_forward(normed, pieces[proj_index])
        joined = dense_qkv[:, proj_index * width : (proj_index + 1) * width] + extra
        projected.append(joined.astype(jnp.bfloat16).reshape(heads_shape))
        stored_qkv.append(stored)
    queries, key_heads, value_heads = projected

    def forward_one(packed):
        return attend_sequence(packed[0], packed[1], packed[2], packed[3], offset_bias)

    attended_heads, log_totals = lax.map(forward_one, (queries, key_heads, value_heads, lengths))
    attended = attended_heads.reshape(-1, width)
    extra_out, stored_out = adapter_forward(attended, pieces[3])
    branch = jnp.dot(attended, w_out, preferred_element_type=jnp.float32) + extra_out
    middle = inputs + branch
    normed_ff_full, inv_ff = rms_forward(middle, gain_ff)
    normed_ff = normed_ff_full.astype(jnp.bfloat16)
    extra_in, stored_in = adapter_forward(normed_ff, pieces[4])
    hidden = jnp.dot(normed_ff, w_in, preferred_element_type=jnp.float32) + extra_in
    active = gelu_smooth(hidden).astype(jnp.bfloat16)
    extra_down, stored_down = adapter_forward(active, pieces[5])
    feed_out = jnp.dot(active, w_down, preferred_element_type=jnp.float32) + extra_down
    output = middle + feed_out
    valid_rows = (
        (jnp.arange(seq_len)[None, :] < lengths[:, None]).astype(jnp.float32).reshape(-1, 1)
    )
    squares = jnp.stack(
        [jnp.sum(valid_rows * member * member) for member in (inputs, branch, feed_out, output)]
    )
    totals, token_count = lax.psum((squares, jnp.sum(lengths).astype(jnp.float32)), ("dp", "fsdp"))
    root_squares = jnp.sqrt(totals / (token_count * width))
    back_pieces = unpack_adapters(lax.all_gather(adapters, ("dp", "fsdp"), axis=0, tiled=True))
    grad_feed = cotangent.reshape(-1, width)
    grad_active, grads_down = adapter_backward(active, back_pieces[5], stored_down, grad_feed)
    grad_active = grad_active + jnp.dot(grad_feed, w_down.T, preferred_element_type=jnp.float32)
    grad_hidden = (grad_active * gelu_slope(hidden)).astype(jnp.bfloat16)
    grad_normed_ff, grads_in = adapter_backward(normed_ff, back_pieces[4], stored_in, grad_hidden)
    grad_normed_ff = grad_normed_ff + jnp.dot(
        grad_hidden, w_in.T, preferred_element_type=jnp.float32
    )
    grad_middle = grad_feed.astype(jnp.float32) + rms_backward(
        middle, gain_ff, inv_ff, grad_normed_ff
    )
    grad_branch = grad_middle.astype(jnp.bfloat16)
    grad_attended, grads_out = adapter_backward(attended, back_pieces[3], stored_out, grad_branch)
    grad_attended = (
        grad_attended + jnp.dot(grad_branch, w_out.T, preferred_element_type=jnp.float32)
    ).astype(jnp.bfloat16)

    def backward_one(packed):
        return attend_backward(
            packed[0], packed[1], packed[2], packed[3], offset_bias, packed[4], packed[5]
        )

    grad_heads = lax.map(
        backward_one,
        (queries, key_heads, value_heads, lengths, log_totals, grad_attended.reshape(heads_shape)),
    )
    grad_parts = [member.reshape(-1, width) for member in grad_heads]
    grad_qkv = jnp.concatenate(grad_parts, axis=1)
    grad_normed = jnp.dot(grad_qkv, w_qkv.T, preferred_element_type=jnp.float32)
    grad_sets = []
    for proj_index in range(3):
        extra_grad, grads_proj = adapter_backward(
            normed, back_pieces[proj_index], stored_qkv[proj_index], grad_parts[proj_index]
        )
        grad_normed = grad_normed + extra_grad
        grad_sets.append(grads_proj)
    grad_sets = grad_sets + [grads_out, grads_in, grads_down]
    grad_inputs = grad_middle + rms_backward(inputs, gain_attn, inv_attn, grad_normed)
    flat_grad = jnp.concatenate([member.reshape(-1) for group in grad_sets for member in group])
    grad_shard = lax.psum_scatter(flat_grad, ("dp", "fsdp"), scatter_dimension=0, tiled=True)
    block_out = output.astype(jnp.bfloat16).reshape(seq_count, seq_len, width)
    tokens_grad = grad_inputs.reshape(seq_count, seq_len, width)
    return (block_out, tokens_grad, grad_shard, root_squares)


def solution(mesh):
    placed = (
        P(("dp", "fsdp"), None, None),
        P(("dp", "fsdp")),
        P(),
        P(),
        P(),
        P(),
        P(),
        P(),
        P(),
        P(),
        P(("dp", "fsdp")),
        P(("dp", "fsdp"), None, None),
    )
    return jax.shard_map(
        per_device,
        mesh=mesh,
        in_specs=placed,
        out_specs=(
            P(("dp", "fsdp"), None, None),
            P(("dp", "fsdp"), None, None),
            P(("dp", "fsdp")),
            P(),
        ),
        check_vma=False,
    )
```

profile of v0, /device:TPU:0, one launch (start us, length us, event | category | flops | bytes accessed | tf_op | source)
XLA Modules:
  0.0 4970.0 jit_solution(12057344834675444559)
XLA Ops:
  33.1 1898.6 %gather_fusion = f32[524288,12]{1,0:T(8,128)} fusion(f32[12,2047]{0,1:T(8,128)} %copy.77, s32[524288]{0:T(1024)} %broadcast_clamp_fusion.1), kind=kCustom, calls=%fused_computation.clone | custom fusion | bytes 52428800 | tf_op jit(solution)/shard_map/while/body/eval_jaxpr/jit(_take)/gather | solution.py:95
  1931.7 144.2 %copy.116 = f32[512,1024,12]{1,0,2:T(8,128)} copy(f32[512,1024,12]{2,1,0:T(8,128)} %bitcast.7) | data formatting | bytes 50331648 | tf_op jit(solution)/shard_map/while/body/eval_jaxpr/jit(_take)/gather | solution.py:95
  2079.5 1898.6 %gather_fusion.1 = f32[524288,12]{1,0:T(8,128)} fusion(f32[12,2047]{0,1:T(8,128)} %copy.77, s32[524288]{0:T(1024)} %broadcast_clamp_fusion), kind=kCustom, calls=%fused_computation.1.clone | custom fusion | bytes 52428800 | tf_op jit(solution)/shard_map/while/body/eval_jaxpr/jit(_take)/gather | solution.py:95
  3978.1 144.1 %copy.117 = f32[512,1024,12]{1,0,2:T(8,128)} copy(f32[512,1024,12]{2,1,0:T(8,128)} %bitcast.11) | data formatting | bytes 50331648 | tf_op jit(solution)/shard_map/while/body/eval_jaxpr/jit(_take)/gather | solution.py:95
  4124.8 10.1 fusion.88
  4134.9 8.2 fusion.156
  4205.9 17.6 fusion.151
  4223.5 11.1 fusion.6
  4235.2 11.3 fusion.106
  4248.8 17.9 fusion.150
  4266.7 11.1 fusion.7
  4277.8 11.3 fusion.107
  4324.3 10.6 fusion.158
  4344.6 10.5 multiply_convert_fusion.2
  4355.1 10.3 fusion.159
  4392.4 7.7 fusion.161
  4400.1 18.5 fusion.24
  4418.5 10.1 fusion.163
  4460.6 10.1 fusion.165
  4470.7 45.2 fusion.100
  4515.9 45.9 fusion.32
  4561.9 5.9 fusion.188
  4567.8 5.9 fusion.187
  4582.3 10.1 fusion.166
  4592.5 12.0 fusion.14
  4604.4 45.2 fusion.103
  4666.7 46.4 add_convert_fusion.1
  4731.8 10.8 add_convert_fusion
  4823.0 14.5 fusion.64
  4840.4 42.6 all-reduce.2
  4883.7 7.6 fusion.60
  4898.6 62.7 %all-reduce.8.cloned.1.call-done = f32[622080]{0:T(1024)} async-done(((f32[622080]{0:T(1024)}), f32[622080]{0:T(1024)}) %all-reduce.8.cloned.1.call-update) | async-done | bytes 2488336
  (439 shorter events, 336.9 us)
Async XLA Ops:
  7.2 4127.8 %copy-start = (bf16[768,2304]{1,0:T(8,128)(2,1)S(1)}, bf16[768,2304]{1,0:T(8,128)(2,1)}, u32[]{:S(2)}) copy-start(bf16[768,2304]{1,0:T(8,128)(2,1)} %param.20) | copy-start | bytes 10616836
  7.2 4136.0 %all-reduce.6.cloned.1.call-start = ((), (), s32[]{:S(2)}) async-start(), calls=%async_computation | async-start | bytes 2490368
  10.3 4951.0 %all-reduce.8.cloned.1.call-start = ((), (), s32[]{:S(2)}) async-start(), calls=%async_computation.1 | async-start | bytes 4980736
  4223.5 11.1 copy-start.80
  4223.5 11.7 copy-start.15
  4266.7 11.1 copy-start.16
  4266.7 11.1 copy-start.79
  4307.8 7.9 copy-start.109
  4344.6 10.5 copy-start.77
  4355.1 10.3 copy-start.6
  4355.1 10.3 copy-start.31
  4418.5 10.1 copy-start.19
  4418.5 10.1 copy-start.48
  4418.5 10.1 copy-start.52
  4418.5 10.1 copy-start.67
  4561.9 13.2 slice-start
  4582.3 10.1 copy-start.88
  4715.8 9.1 copy-start.90
  4715.8 9.1 copy-start.96
  4731.8 10.9 copy-start.49
  4731.8 10.9 copy-start.68
  4731.8 10.9 copy-start.71
  4731.8 12.1 copy-start.37
  4743.9 8.1 copy-start.92
  4743.9 8.1 copy-start.98
  4796.3 20.2 copy-start.87
  4796.3 21.6 copy-start.36
  4796.3 23.5 copy-start.76
  4796.3 25.0 copy-start.75
  4823.0 60.8 %copy-start.104 = (f32[1024]{0:T(1024)S(1)}, f32[1024]{0:T(1024)}, u32[]{:S(2)}) copy-start(f32[1024]{0:T(1024)} %copy-done.103) | copy-start | bytes 12292
  4823.0 60.7 %copy-start.106 = (f32[1024]{0:T(1024)S(1)}, f32[1024]{0:T(1024)}, u32[]{:S(2)}) copy-start(f32[1024]{0:T(1024)} %get-tuple-element.123) | copy-start | bytes 12292
  4823.0 60.7 %copy-start.108 = (f32[1024]{0:T(1024)S(1)}, f32[1024]{0:T(1024)}, u32[]{:S(2)}) copy-start(f32[1024]{0:T(1024)} %copy-done.107) | copy-start | bytes 12292
  (89 other events, 328.8 us)
Sparse Core Ops, SparseCore 0:
  13.4 133.2 all-reduce.5
  4823.1 138.2 all-reduce.7
where the time goes:
time: 5060 us; the launch traced here: 4970 us
  local copies, waits for them, and re-layouts  4260 us (84%)
  matrix products  505 us (10%)
  other arithmetic  84.2 us (2%)
  waiting for transfers between devices  62.8 us (1%)
    gather x4, local copies, waits for them, and re-layouts, block_bias(): gathered = jnp.take(offset_bias, offsets, axis=1)  4090 us
  transfers between devices with their start and end apart: 2, of which 1 were waited for; matrix products, arithmetic and copies ran while one was open for 84% of the time, Pallas kernels for 0%

commit v1 on v0

v1 whole, which is shorter than its diff:
```python
import functools

import jax
import jax.numpy as jnp
from jax import lax
from jax.experimental import pallas as pl
from jax.experimental.pallas import tpu as pltpu
from jax.sharding import PartitionSpec as P

D = 768
FF = 3072
HEADS = 12
HDIM = 64
EXPERTS = 10
RANK = 4
COLS = EXPERTS * RANK
LANES = 128

EPSILON = 1e-06
MASKED = -1000000000.0
GELU_SCALE = 0.7978845608028654
GELU_CUBIC = 0.044715
LOG2E = 1.4426950408889634
LN2 = 0.6931471805599453
QUERY_SCALE = 0.125 * LOG2E

ROWS = 256
QBLOCK = 256
VMEM_BYTES = 60 * 1024 * 1024

F32 = jnp.float32
BF16 = jnp.bfloat16


def dot(a, b):
    return lax.dot_general(a, b, (((1,), (0,)), ((), ())), preferred_element_type=F32)


def dot_nt(a, b):
    return lax.dot_general(a, b, (((1,), (1,)), ((), ())), preferred_element_type=F32)


def dot_tn(a, b):
    return lax.dot_general(a, b, (((0,), (0,)), ((), ())), preferred_element_type=F32)


def lane_iota(shape):
    return lax.broadcasted_iota(jnp.int32, shape, 1)


def row_iota(shape):
    return lax.broadcasted_iota(jnp.int32, shape, 0)


def gates_of(logits, groups):
    lane = lane_iota(logits.shape)
    result = jnp.zeros_like(logits)
    for group in range(groups):
        inside = (lane >= group * COLS) & (lane < (group + 1) * COLS)
        peak = jnp.max(jnp.where(inside, logits, -jnp.inf), axis=-1, keepdims=True)
        weights = jnp.where(inside, jnp.exp(logits - peak), 0.0)
        total = jnp.sum(weights, axis=-1, keepdims=True)
        result = result + weights * (4.0 / total)
    return result


def gate_grads(grad_mixed, lowrank, gates, groups):
    lane = lane_iota(gates.shape)
    grad_rank = grad_mixed * gates
    product = grad_mixed * lowrank
    summed = product
    for step in range(1, RANK):
        summed = summed + pltpu.roll(product, LANES - step, 1)
    weighted = gates * product
    centre = jnp.zeros_like(gates)
    for group in range(groups):
        inside = (lane >= group * COLS) & (lane < (group + 1) * COLS)
        part = jnp.sum(jnp.where(inside, weighted, 0.0), axis=-1, keepdims=True)
        centre = centre + jnp.where(inside, part, 0.0)
    grad_logits = jnp.where(lane % RANK == 0, gates * (summed - centre), 0.0)
    return grad_rank, grad_logits


def single_forward(inputs, ar_ref):
    packed = dot(inputs, ar_ref[...])
    lane = lane_iota(packed.shape)
    gates = gates_of(pltpu.roll(packed, 64, 1), 1)
    lowrank = jnp.where(lane < COLS, packed, 0.0)
    return lowrank, gates, (lowrank * gates).astype(BF16)


def single_backward(grad_mixed, lowrank, gates):
    grad_rank, grad_logits = gate_grads(grad_mixed, lowrank, gates, 1)
    return (grad_rank + pltpu.roll(grad_logits, 64, 1)).astype(BF16)


def rms_inverse(values):
    return lax.rsqrt(jnp.mean(values * values, axis=-1, keepdims=True) + EPSILON)


def rms_backward(values, gain, inverse, grad_normed):
    weighted = grad_normed * gain
    return inverse * weighted - values * (
        inverse * inverse * inverse * jnp.mean(values * weighted, axis=-1, keepdims=True)
    )


def params(**more):
    return pltpu.CompilerParams(vmem_limit_bytes=VMEM_BYTES, **more)


def whole(shape):
    zeros = (0,) * len(shape)
    return pl.BlockSpec(shape, lambda *_: zeros)


def project_kernel(
    x_ref, gain_ref, w_ref, ar_ref, b_ref, qt_ref, k_ref, kt_ref, v_ref, vt_ref, zg_ref
):
    values = x_ref[...].astype(F32)
    normed = (values * rms_inverse(values) * gain_ref[...]).astype(BF16)
    packed = dot(normed, ar_ref[...])
    lowrank = packed[:, :LANES]
    gates = gates_of(packed[:, LANES:], 3)
    zg_ref[:, :LANES] = lowrank
    zg_ref[:, LANES:] = gates
    mixed = (lowrank * gates).astype(BF16)
    for index in range(3):
        columns = slice(index * D, (index + 1) * D)
        part = dot(normed, w_ref[:, columns]) + dot(mixed, b_ref[:, columns])
        if index == 0:
            qt_ref[...] = (part * QUERY_SCALE).astype(BF16).T
        else:
            low = part.astype(BF16)
            natural, turned = ((k_ref, kt_ref), (v_ref, vt_ref))[index - 1]
            natural[...] = low
            turned[...] = low.T


def project(x, gain, w_qkv, ar_qkv, b_qkv):
    length = x.shape[0]
    tile = pl.BlockSpec((ROWS, D), lambda i: (i, 0))
    turned = pl.BlockSpec((D, ROWS), lambda i: (0, i))
    natural_shape = jax.ShapeDtypeStruct((length, D), BF16)
    turned_shape = jax.ShapeDtypeStruct((D, length), BF16)
    return pl.pallas_call(
        project_kernel,
        grid=(length // ROWS,),
        in_specs=[
            tile,
            whole((1, D)),
            whole(w_qkv.shape),
            whole(ar_qkv.shape),
            whole(b_qkv.shape),
        ],
        out_specs=[
            turned,
            tile,
            turned,
            tile,
            turned,
            pl.BlockSpec((ROWS, 2 * LANES), lambda i: (i, 0)),
        ],
        out_shape=[
            turned_shape,
            natural_shape,
            turned_shape,
            natural_shape,
            turned_shape,
            jax.ShapeDtypeStruct((length, 2 * LANES), F32),
        ],
        compiler_params=params(),
        name="project",
    )(x, gain, w_qkv, ar_qkv, b_qkv)


def bias_table(offset_row, length):
    spread = jnp.broadcast_to(offset_row, (LANES, 2 * length))
    return pltpu.roll(spread, 2 * length - (LANES - 1), 1, stride=1, stride_axis=0)


def add_bias(scores, table_ref, start, length):
    width = scores.shape[1]
    parts = []
    for block in range(length // LANES):
        offset = start - LANES * block + (length - LANES)
        parts.append(
            scores[block * LANES : (block + 1) * LANES] + table_ref[:, offset : offset + width]
        )
    return jnp.concatenate(parts, axis=0)


def key_extras(length_ref, shape, odd):
    lane = lane_iota(shape) - (0 if odd else HDIM)
    invalid = row_iota(shape) >= length_ref[0]
    extras = jnp.where((lane == 0) & invalid, MASKED, 0.0)
    return jnp.where((lane >= 1) & (lane <= 3), 1.0, extras).astype(BF16)


def head_lanes(odd):
    lane = lane_iota((1, LANES))
    return ((lane >= HDIM) if odd else (lane < HDIM)).astype(F32).astype(BF16)


def extra_rows(rows):
    width = rows[0].shape[1]
    index = row_iota((8, width))
    block = jnp.zeros((8, width), F32)
    for place, row in enumerate(rows):
        block = jnp.where(index == place, row, block)
    return jnp.concatenate([block, jnp.zeros((HDIM - 8, width), F32)], axis=0).astype(BF16)


def split_three(row):
    high = row.astype(BF16).astype(F32)
    middle = (row - high).astype(BF16).astype(F32)
    return high, middle, row - high - middle


def join_rows(rows, extras, odd):
    return jnp.concatenate([extras, rows] if odd else [rows, extras], axis=0)


def attend_kernel(length_ref, off_ref, qt_ref, k_ref, vt_ref, o_ref, lse_ref, table, key_more):
    length = k_ref.shape[0]

    @pl.when(pl.program_id(0) == 0)
    def _():
        for odd in range(2):
            key_more[odd] = key_extras(length_ref, k_ref.shape, odd)

    for odd in range(2):
        half = slice(odd * HDIM, (odd + 1) * HDIM)
        table[odd] = bias_table(off_ref[0, odd : odd + 1, :], length)
        keys = k_ref[...] * head_lanes(odd) + key_more[odd]
        ones = jnp.ones((1, length), F32)
        queries = join_rows(qt_ref[half, :], extra_rows([ones]), odd)
        values = jnp.concatenate([vt_ref[half, :], jnp.ones((16, length), BF16)], axis=0)
        for start in range(0, length, QBLOCK):
            columns = slice(start, start + QBLOCK)
            scores = add_bias(dot(keys, queries[:, columns]), table.at[odd], start, length)
            peak = jnp.max(scores, axis=0, keepdims=True)
            weights = jnp.exp2(scores - peak).astype(BF16)
            summed = dot(values, weights)
            total = summed[HDIM : HDIM + 1]
            o_ref[half, columns] = (summed[:HDIM] / total).astype(BF16)
            lse_ref[0, odd : odd + 1, columns] = peak + jnp.log2(total)


def attend(length_valid, offsets, qt, k, vt):
    length = k.shape[0]
    turned = pl.BlockSpec((LANES, length), lambda p: (p, 0))
    natural = pl.BlockSpec((length, LANES), lambda p: (0, p))
    pair_rows = pl.BlockSpec((1, 2, 2 * length), lambda p: (p, 0, 0))
    return pl.pallas_call(
        attend_kernel,
        grid=(HEADS // 2,),
        in_specs=[
            pl.BlockSpec(memory_space=pltpu.SMEM),
            pair_rows,
            turned,
            natural,
            turned,
        ],
        out_specs=[turned, pl.BlockSpec((1, 2, length), lambda p: (p, 0, 0))],
        out_shape=[
            jax.ShapeDtypeStruct((D, length), BF16),
            jax.ShapeDtypeStruct((HEADS // 2, 2, length), F32),
        ],
        scratch_shapes=[
            pltpu.VMEM((2, LANES, 2 * length), F32),
            pltpu.VMEM((2, length, LANES), BF16),
        ],
        compiler_params=params(),
        name="attend",
    )(length_valid, offsets, qt, k, vt)


def attend_back_kernel(
    length_ref,
    off_ref,
    qt_ref,
    k_ref,
    kt_ref,
    v_ref,
    ot_ref,
    gt_ref,
    lse_ref,
    dq_ref,
    dk_ref,
    dv_ref,
    table,
    key_more,
    weights_all,
    grads_all,
):
    length = k_ref.shape[0]

    @pl.when(pl.program_id(0) == 0)
    def _():
        for odd in range(2):
            key_more[odd] = key_extras(length_ref, k_ref.shape, odd)

    lane = lane_iota((1, LANES))
    first_lanes = lane < HDIM
    grad_query_parts = []
    for odd in range(2):
        half = slice(odd * HDIM, (odd + 1) * HDIM)
        table[odd] = bias_table(off_ref[0, odd : odd + 1, :], length)
        keys = k_ref[...] * head_lanes(odd) + key_more[odd]
        place = lane - (0 if odd else HDIM)
        value_more = ((place >= 0) & (place < 3)).astype(F32).astype(BF16)
        values = v_ref[...] * head_lanes(odd) + value_more
        ones = jnp.ones((1, length), F32)
        lse = lse_ref[0, odd : odd + 1, :]
        queries = join_rows(
            qt_ref[half, :], extra_rows([ones] + [-part for part in split_three(lse)]), odd
        )
        delta = jnp.sum(
            ot_ref[half, :].astype(F32) * gt_ref[half, :].astype(F32), axis=0, keepdims=True
        )
        grads = join_rows(
            gt_ref[half, :], extra_rows([-part for part in split_three(delta)]), odd
        )
        for start in range(0, length, QBLOCK):
            columns = slice(start, start + QBLOCK)
            scores = add_bias(dot(keys, queries[:, columns]), table.at[odd], start, length)
            weights = jnp.exp2(scores)
            weights_all[:, columns] = weights.astype(BF16)
            grad_scores = weights * dot(values, grads[:, columns])
            grads_all[:, columns] = grad_scores.astype(BF16)
        grad_query_parts.append(dot(kt_ref[half, :], grads_all[...]) * 0.125)
        grad_values = dot_nt(weights_all[...], gt_ref[...])
        grad_keys = dot_nt(grads_all[...], qt_ref[...]) * LN2
        if odd:
            dv_ref[...] = jnp.where(first_lanes, even_values, grad_values).astype(BF16)
            dk_ref[...] = jnp.where(first_lanes, even_keys, grad_keys).astype(BF16)
        else:
            even_values, even_keys = grad_values, grad_keys
    dq_ref[...] = jnp.concatenate(grad_query_parts, axis=0).T.astype(BF16)


def attend_back(length_valid, offsets, qt, k, kt, v, ot, gt, lse):
    length = k.shape[0]
    turned = pl.BlockSpec((LANES, length), lambda p: (p, 0))
    natural = pl.BlockSpec((length, LANES), lambda p: (0, p))
    pair_rows = pl.BlockSpec((1, 2, 2 * length), lambda p: (p, 0, 0))
    natural_shape = jax.ShapeDtypeStruct((length, D), BF16)
    return pl.pallas_call(
        attend_back_kernel,
        grid=(HEADS // 2,),
        in_specs=[
            pl.BlockSpec(memory_space=pltpu.SMEM),
            pair_rows,
            turned,
            natural,
            turned,
            natural,
            turned,
            turned,
            pl.BlockSpec((1, 2, length), lambda p: (p, 0, 0)),
        ],
        out_specs=[natural] * 3,
        out_shape=[natural_shape] * 3,
        scratch_shapes=[
            pltpu.VMEM((2, LANES, 2 * length), F32),
            pltpu.VMEM((2, length, LANES), BF16),
            pltpu.VMEM((length, length), BF16),
            pltpu.VMEM((length, length), BF16),
        ],
        compiler_params=params(),
        name="attend_back",
    )(length_valid, offsets, qt, k, kt, v, ot, gt, lse)


def middle_kernel(
    length_ref,
    ot_ref,
    x_ref,
    cot_ref,
    gain_ref,
    w_out_ref,
    w_in_ref,
    w_down_ref,
    ar_out_ref,
    b_out_ref,
    ar_in_ref,
    b_in_ref,
    ar_down_ref,
    b_down_ref,
    out_ref,
    dmid_ref,
    gt_ref,
    sums_ref,
    dar_out_ref,
    db_out_ref,
    dar_in_ref,
    db_in_ref,
    dar_down_ref,
    db_down_ref,
):
    step = pl.program_id(0)

    @pl.when(step == 0)
    def _():
        for ref in (
            sums_ref,
            dar_out_ref,
            db_out_ref,
            dar_in_ref,
            db_in_ref,
            dar_down_ref,
            db_down_ref,
        ):
            ref[...] = jnp.zeros_like(ref)

    attended = ot_ref[...].T
    inputs = x_ref[...].astype(F32)
    gain = gain_ref[...]
    low_out, gates_out, mixed_out = single_forward(attended, ar_out_ref)
    branch = dot(attended, w_out_ref[...]) + dot(mixed_out, b_out_ref[...])
    middle = inputs + branch
    inverse = rms_inverse(middle)
    normed = (middle * inverse * gain).astype(BF16)
    low_in, gates_in, mixed_in = single_forward(normed, ar_in_ref)
    hidden = dot(normed, w_in_ref[...]) + dot(mixed_in, b_in_ref[...])
    square = hidden * hidden
    tangent = jnp.tanh(hidden * (GELU_SCALE + (GELU_SCALE * GELU_CUBIC) * square))
    half = 0.5 + 0.5 * tangent
    smooth = hidden * half
    slope = half + smooth * (1.0 - tangent) * (
        GELU_SCALE + (3.0 * GELU_SCALE * GELU_CUBIC) * square
    )
    active = smooth.astype(BF16)
    low_down, gates_down, mixed_down = single_forward(active, ar_down_ref)
    feed = dot(active, w_down_ref[...]) + dot(mixed_down, b_down_ref[...])
    output = middle + feed
    out_ref[...] = output.astype(BF16)

    rows = row_iota((ROWS, 1)) + step * ROWS
    valid = (rows < length_ref[0]).astype(F32)
    lane = lane_iota((8, LANES))
    totals = jnp.zeros((8, LANES), F32)
    for place, member in enumerate((inputs, branch, feed, output)):
        kept = member * valid
        totals = jnp.where(lane == place, jnp.sum(kept * kept), totals)
    sums_ref[...] += totals

    cot = cot_ref[...]
    delta_down = single_backward(dot_nt(cot, b_down_ref[...]), low_down, gates_down)
    grad_active = dot_nt(cot, w_down_ref[...]) + dot_nt(delta_down, ar_down_ref[...])
    grad_hidden = (grad_active * slope).astype(BF16)
    dar_down_ref[...] += dot_tn(delta_down, active)
    db_down_ref[...] += dot_tn(mixed_down, cot)

    delta_in = single_backward(dot_nt(grad_hidden, b_in_ref[...]), low_in, gates_in)
    grad_normed = dot_nt(grad_hidden, w_in_ref[...]) + dot_nt(delta_in, ar_in_ref[...])
    dar_in_ref[...] += dot_tn(delta_in, normed)
    db_in_ref[...] += dot_tn(mixed_in, grad_hidden)

    grad_middle = cot.astype(F32) + rms_backward(middle, gain, inverse, grad_normed)
    dmid_ref[...] = grad_middle
    grad_branch = grad_middle.astype(BF16)
    delta_out = single_backward(dot_nt(grad_branch, b_out_ref[...]), low_out, gates_out)
    grad_attended = dot_nt(grad_branch, w_out_ref[...]) + dot_nt(delta_out, ar_out_ref[...])
    gt_ref[...] = grad_attended.astype(BF16).T
    dar_out_ref[...] += dot_tn(delta_out, attended)
    db_out_ref[...] += dot_tn(mixed_out, grad_branch)


def middle_part(length_valid, ot, x, cot, gain, w_out, w_in, w_down, adapters):
    length = x.shape[0]
    tile = pl.BlockSpec((ROWS, D), lambda i: (i, 0))
    turned = pl.BlockSpec((D, ROWS), lambda i: (0, i))
    grad_shapes = [
        jax.ShapeDtypeStruct((LANES, width), F32) for width in (D, D, D, FF, FF, D)
    ]
    out_shape = [
        jax.ShapeDtypeStruct((length, D), BF16),
        jax.ShapeDtypeStruct((length, D), F32),
        jax.ShapeDtypeStruct((D, length), BF16),
        jax.ShapeDtypeStruct((8, LANES), F32),
    ] + grad_shapes
    return pl.pallas_call(
        middle_kernel,
        grid=(length // ROWS,),
        in_specs=[pl.BlockSpec(memory_space=pltpu.SMEM), turned, tile, tile]
        + [whole(member.shape) for member in (gain, w_out, w_in, w_down, *adapters)],
        out_specs=[tile, tile, turned] + [whole(member.shape) for member in out_shape[3:]],
        out_shape=out_shape,
        compiler_params=params(),
        name="middle_part",
    )(length_valid, ot, x, cot, gain, w_out, w_in, w_down, *adapters)


def project_back_kernel(
    x_ref,
    gain_ref,
    w_ref,
    ar_ref,
    b_ref,
    zg_ref,
    dq_ref,
    dk_ref,
    dv_ref,
    dmid_ref,
    out_ref,
    dar_ref,
    db_ref,
):
    @pl.when(pl.program_id(0) == 0)
    def _():
        dar_ref[...] = jnp.zeros_like(dar_ref)
        db_ref[...] = jnp.zeros_like(db_ref)

    values = x_ref[...].astype(F32)
    gain = gain_ref[...]
    inverse = rms_inverse(values)
    normed = (values * inverse * gain).astype(BF16)
    lowrank = zg_ref[:, :LANES]
    gates = zg_ref[:, LANES:]
    mixed = (lowrank * gates).astype(BF16)
    grads = (dq_ref[...], dk_ref[...], dv_ref[...])
    grad_normed = jnp.zeros((ROWS, D), F32)
    grad_mixed = jnp.zeros((ROWS, LANES), F32)
    for index, grad in enumerate(grads):
        columns = slice(index * D, (index + 1) * D)
        grad_mixed = grad_mixed + dot_nt(grad, b_ref[:, columns])
        grad_normed = grad_normed + dot_nt(grad, w_ref[:, columns])
        db_ref[:, columns] += dot_tn(mixed, grad)
    grad_rank, grad_logits = gate_grads(grad_mixed, lowrank, gates, 3)
    delta = jnp.concatenate([grad_rank, grad_logits], axis=1).astype(BF16)
    grad_normed = grad_normed + dot_nt(delta, ar_ref[...])
    dar_ref[...] += dot_tn(delta, normed)
    out_ref[...] = dmid_ref[...] + rms_backward(values, gain, inverse, grad_normed)


def project_back(x, gain, w_qkv, ar_qkv, b_qkv, zg, dq, dk, dv, dmid):
    length = x.shape[0]
    tile = pl.BlockSpec((ROWS, D), lambda i: (i, 0))
    out_shape = [
        jax.ShapeDtypeStruct((length, D), F32),
        jax.ShapeDtypeStruct((2 * LANES, D), F32),
        jax.ShapeDtypeStruct((LANES, 3 * D), F32),
    ]
    return pl.pallas_call(
        project_back_kernel,
        grid=(length // ROWS,),
        in_specs=[
            tile,
            whole((1, D)),
            whole(w_qkv.shape),
            whole(ar_qkv.shape),
            whole(b_qkv.shape),
            pl.BlockSpec((ROWS, 2 * LANES), lambda i: (i, 0)),
            tile,
            tile,
            tile,
            tile,
        ],
        out_specs=[tile] + [whole(member.shape) for member in out_shape[1:]],
        out_shape=out_shape,
        compiler_params=params(),
        name="project_back",
    )(x, gain, w_qkv, ar_qkv, b_qkv, zg, dq, dk, dv, dmid)


def unpack_adapters(flat_values):
    result = []
    offset = 0
    for fan_in, fan_out in ((D, D), (D, D), (D, D), (D, D), (D, FF), (FF, D)):
        members = []
        for form in ((fan_in, COLS), (COLS, fan_out), (fan_in, EXPERTS)):
            count = form[0] * form[1]
            members.append(flat_values[offset : offset + count].reshape(form))
            offset += count
        result.append(tuple(members))
    return result


def pack_single(piece):
    down, up, router = piece
    wide = jnp.repeat(router, RANK, axis=1)
    zeros = jnp.zeros((down.shape[0], 64 - COLS), down.dtype)
    packed = jnp.concatenate([down, zeros, wide, zeros], axis=1)
    return packed, jnp.pad(up, ((0, LANES - COLS), (0, 0)))


def pack_three(pieces):
    zeros = jnp.zeros((D, LANES - 3 * COLS), pieces[0][0].dtype)
    packed = jnp.concatenate(
        [piece[0] for piece in pieces]
        + [zeros]
        + [jnp.repeat(piece[2], RANK, axis=1) for piece in pieces]
        + [zeros],
        axis=1,
    )
    ups = [
        jnp.pad(piece[1], ((index * COLS, LANES - (index + 1) * COLS), (0, 0)))
        for index, piece in enumerate(pieces)
    ]
    return packed, jnp.concatenate(ups, axis=1)


def per_device(
    tokens,
    lengths,
    buckets,
    rel_table,
    gain_attn,
    gain_ff,
    w_qkv,
    w_out,
    w_in,
    w_down,
    adapters,
    cotangent,
    axes,
):
    seq_count, length, width = tokens.shape
    x = tokens.reshape(length, width)
    cot = cotangent.reshape(length, width)
    pieces = unpack_adapters(lax.all_gather(adapters, axes, axis=0, tiled=True))
    gain_first = gain_attn.reshape(1, width)
    gain_second = gain_ff.reshape(1, width)

    reversed_buckets = jnp.pad(buckets[::-1], (0, 1))
    hits = (jnp.arange(rel_table.shape[0])[:, None] == reversed_buckets[None, :]).astype(F32)
    offsets = jnp.dot(rel_table.T * LOG2E, hits, precision=lax.Precision.HIGHEST)
    offsets = offsets.reshape(HEADS // 2, 2, 2 * length)

    ar_qkv, b_qkv = pack_three(pieces[:3])
    rest = [member for piece in pieces[3:] for member in pack_single(piece)]

    qt, k, kt, v, vt, zg = project(x, gain_first, w_qkv, ar_qkv, b_qkv)
    ot, lse = attend(lengths, offsets, qt, k, vt)
    block_out, dmid, gt, sums, *grads = middle_part(
        lengths, ot, x, cot, gain_second, w_out, w_in, w_down, rest
    )
    totals, token_count = lax.psum((sums[0, :4], jnp.sum(lengths).astype(F32)), axes)
    root_squares = jnp.sqrt(totals / (token_count * width))
    dq, dk, dv = attend_back(lengths, offsets, qt, k, kt, v, ot, gt, lse)
    tokens_grad, dar_qkv, db_qkv = project_back(
        x, gain_first, w_qkv, ar_qkv, b_qkv, zg, dq, dk, dv, dmid
    )

    flat = []
    for index in range(3):
        first = index * COLS
        flat.append(dar_qkv[first : first + COLS].T)
        flat.append(db_qkv[first : first + COLS, index * D : (index + 1) * D])
        flat.append(dar_qkv[LANES + first : LANES + first + COLS : RANK].T)
    for index in range(3):
        dar, db = grads[2 * index], grads[2 * index + 1]
        flat.append(dar[:COLS].T)
        flat.append(db[:COLS])
        flat.append(dar[64 : 64 + COLS : RANK].T)
    flat_grad = jnp.concatenate([member.reshape(-1) for member in flat])
    grad_shard = lax.psum_scatter(flat_grad, axes, scatter_dimension=0, tiled=True)
    return (
        block_out.reshape(tokens.shape),
        tokens_grad.reshape(tokens.shape),
        grad_shard,
        root_squares,
    )


def solution(mesh):
    axes = tuple(mesh.axis_names)
    sequence = P(axes, None, None)
    placed = (
        sequence,
        P(axes),
        P(),
        P(),
        P(),
        P(),
        P(),
        P(),
        P(),
        P(),
        P(axes),
        sequence,
    )
    return jax.shard_map(
        functools.partial(per_device, axes=axes),
        mesh=mesh,
        in_specs=placed,
        out_specs=(sequence, sequence, P(axes), P()),
        check_vma=False,
    )
```

time: 5060 us -> 539 us (0.11); the launches traced: 4970 us -> 532 us
  local copies, waits for them, and re-layouts: 4260 us -> 75.2 us
  matrix products: 505 us -> 0.21 us
  Pallas kernels: 0 us -> 166 us
  waiting for transfers between devices: 62.8 us -> 228 us
  other arithmetic: 84.2 us -> 5.21 us
    gather x4 -> x0, local copies, waits for them, and re-layouts: 4090 us -> none  [block_bias(): gathered = jnp.take(offset_bias, offsets, axis=1)]
    dot_general x75 -> x1, matrix products: 505 us -> 0.21 us  [per_device(): jnp.dot(rel_table.T * LOG2E, hits, precision=lax.Precision.HIGHEST)]
    pallas_call x0 -> x5, Pallas kernels: none -> 166 us  [the longest x1 70.6 us: middle_part(): pl.pallas_call(middle_kernel, grid=(length // ROWS,), in_specs=[pl.BlockS...]
    unnamed x4, waiting for transfers between devices: 62.8 us -> 228 us
  transfers between devices with their start and end apart: 2 -> 2, of which waited for: 1 -> 2; matrix products, arithmetic and copies ran while one was open for 84% -> 1% of each run, Pallas kernels for 0% -> 0%
where the time goes in v1:
time: 539 us; the launch traced here: 532 us
  waiting for transfers between devices  228 us (42%)
  Pallas kernels  166 us (31%)
  local copies, waits for them, and re-layouts  75.2 us (14%)
  blocking collectives  41.1 us (8%)
  between operations  16.4 us (3%)
    unnamed x4, waiting for transfers between devices  228 us
    pallas_call x1, Pallas kernels, middle_part(): pl.pallas_call(middle_kernel, grid=(length // ROWS,), in_specs=[pl.BlockS...  70.6 us
    psum x1, blocking collectives, per_device(): lax.psum((sums[0, :4], jnp.sum(lengths).astype(F32)), axes)  41.1 us
    pallas_call x1, Pallas kernels, attend_back(): pl.pallas_call(attend_back_kernel, grid=(HEADS // 2,), in_specs=[pl.Block...  34.6 us
    pallas_call x1, Pallas kernels, attend(): pl.pallas_call(attend_kernel, grid=(HEADS // 2,), in_specs=[pl.BlockSpec(...  34.4 us
    unnamed x42, local copies, waits for them, and re-layouts  27.8 us
    pallas_call x1, Pallas kernels, project_back(): pl.pallas_call(project_back_kernel, grid=(length // ROWS,), in_specs=[til...  14.2 us
    pallas_call x1, Pallas kernels, project(): pl.pallas_call(project_kernel, grid=(length // ROWS,), in_specs=[tile, wh...  12.1 us
  transfers between devices with their start and end apart: 2, of which 2 were waited for; matrix products, arithmetic and copies ran while one was open for 1% of the time, Pallas kernels for 0%

profile of v1, /device:TPU:0, one launch (start us, length us, event | category | flops | bytes accessed | tf_op | source)
XLA Modules:
  0.0 531.7 jit_solution(8435153402155091595)
XLA Ops:
  7.3 1.2 dynamic-update-slice
  12.5 134.8 %all-reduce.13.cloned.1.call-done = bf16[622080]{0:T(1024)(128)(2,1)} async-done(((bf16[622080]{0:T(1024)(128)(2,1)}), bf16[622080]{0:T(1024)(128)(2,1)}) %all-reduce.13.cloned.1.call-update) | async-done | bytes 1244176
  147.3 1.8 fusion.13
  160.4 1.8 slice.295
  163.0 1.2 reshape.288
  165.8 1.7 fusion.5.b_ref
  167.6 1.8 pad_maximum_fusion.ar_down_ref
  169.5 2.3 concatenate.18.ar_ref
  171.8 12.1 %project.1 = (bf16[768,1024]{1,0:T(8,128)(2,1)}, bf16[1024,768]{1,0:T(8,128)(2,1)}, bf16[768,1024]{1,0:T(8,128)(2,1)}, bf16[1024,768]{1,0:T(8,128)(2,1)}, bf16[7...) custom-call(bf16[1024,768]{1,0:T(8,128)(2,1)} %bitcast.41, f32[1,768]{1,0:T(1,128)} %reshape.274.gain_ref, ...), custom_call_target="tpu_custom_call" | custom-call | tf_op jit(solution)/shard_map/project/pallas_call | solution.py:146
  183.9 34.4 %attend.1 = (bf16[768,1024]{1,0:T(8,128)(2,1)}, f32[6,2,1024]{2,1,0:T(2,128)}) custom-call(s32[1]{0:T(128)S(6)} %copy.85.length_ref, f32[6,2,2048]{2,1,0:T(2,128)} %reshape.272.off_ref, bf16[768,1024]{1,0:T(8,128)(2,1)} %get-tuple-element.28.qt_ref, bf16[1024,768]{1,0:T(8,128)(2,1)} %get-tuple-element.29.k_ref, bf16[768,1024]{1,0:T(8,128)(2,1)} %get-tuple-element.30.vt_ref), custom_call_target="tpu_custom_call" | custom-call | tf_op jit(solution)/shard_map/attend/pallas_call | solution.py:255
  219.5 70.6 %middle_part.1 = (bf16[1024,768]{1,0:T(8,128)(2,1)}, f32[1024,768]{1,0:T(8,128)}, bf16[768,1024]{1,0:T(8,128)(2,1)}, f32[8,128]{1,0:T(8,128)}, f32[128,768]{1,0:...) custom-call(s32[1]{0:T(128)S(6)} %copy.85.length_ref, ...), custom_call_target="tpu_custom_call" | custom-call | tf_op jit(solution)/shard_map/middle_part/pallas_call | solution.py:484
  290.2 34.6 %attend_back.1 = (bf16[1024,768]{1,0:T(8,128)(2,1)}, bf16[1024,768]{1,0:T(8,128)(2,1)}, bf16[1024,768]{1,0:T(8,128)(2,1)}) custom-call(s32[1]{0:T(128)S(6)} %copy.85.length_ref, f32[6,2,2048]{2,1,0:T(2,128)} %reshape.272.off_ref, bf16[768,1024]{1,0:T(8,128)(2,1)} %get-tuple-element.28.qt_ref, bf16[1024,768]{1,0:T(8,128)(2,1)} %get-tuple-element.29.k_ref, ...), custom_call_target="tpu_custom_call" | custom-call | tf_op jit(solution)/shard_map/attend_back/pallas_call | solution.py:349
  324.8 14.2 %project_back.1 = (f32[1024,768]{1,0:T(8,128)}, f32[256,768]{1,0:T(8,128)}, f32[128,2304]{1,0:T(8,128)}) custom-call(bf16[1024,768]{1,0:T(8,128)(2,1)} %bitcast.43, f32[1,768]{1,0:T(1,128)} %reshape.274.gain_ref, bf16[768,2304]{1,0:T(8,128)(2,1)} %w_ref.3, bf16[768,256]{1,0:T(8,128)(2,1)} %concatenate.18.ar_ref, bf16[128,2304]{1,0:T(8,128)(2,1)} %fusion.5.b_ref, ...), custom_call_target="tpu_custom_call" | custom-call | tf_op jit(solution)/shard_map/project_back/pallas_call | solution.py:546
  346.8 1.3 slice_bitcast_fusion.4
  362.3 1.2 reshape.309
  364.2 1.4 constant_dynamic-update-slice_fusion.15
  365.6 1.6 constant_dynamic-update-slice_fusion.14
  367.2 1.6 constant_dynamic-update-slice_fusion.13
  368.7 1.4 constant_dynamic-update-slice_fusion.12
  370.1 1.6 constant_dynamic-update-slice_fusion.11
  372.3 1.4 constant_dynamic-update-slice_fusion.9
  373.7 1.6 constant_dynamic-update-slice_fusion.8
  375.3 1.6 constant_dynamic-update-slice_fusion.7
  376.9 1.4 constant_dynamic-update-slice_fusion.6
  378.3 1.6 constant_dynamic-update-slice_fusion.5
  380.7 1.4 constant_dynamic-update-slice_fusion.3
  382.1 1.9 constant_dynamic-update-slice_fusion.2
  383.9 1.6 constant_dynamic-update-slice_fusion.1
  385.5 1.6 constant_dynamic-update-slice_fusion
  387.8 41.1 %all-reduce.9 = (f32[4]{0:T(128)S(1)}, f32[]{:T(128)}) all-reduce(f32[4]{0:T(128)S(1)} %slice_bitcast_fusion.7, f32[]{:T(128)} %bitcast.17), channel_id=1, replica_groups=mesh['dp'=8,'fsdp'=4] {'dp','fsdp'}, use_global_device_ids=true, to_apply=%region_1.2 | all-reduce | flops 5 | bytes 40 | tf_op jit(solution)/shard_map/psum | solution.py:640
  430.0 92.7 %all-reduce.15.cloned.1.call-done = f32[622080]{0:T(1024)} async-done(((f32[622080]{0:T(1024)}), f32[622080]{0:T(1024)}) %all-reduce.15.cloned.1.call-update) | async-done | bytes 2488336
  522.7 1.6 dynamic-slice
  (125 shorter events, 43.5 us)
Async XLA Ops:
  7.2 3.1 copy-start.6
  7.2 3.3 copy-start.5
  7.2 4.2 copy-start.7
  7.2 4.8 copy-start.8
  7.2 140.1 %all-reduce.13.cloned.1.call-start = ((), (), s32[]{:S(2)}) async-start(), calls=%async_computation | async-start | bytes 2490368
  8.5 1.0 copy-start
  9.6 513.1 %all-reduce.15.cloned.1.call-start = ((), (), s32[]{:S(2)}) async-start(), calls=%async_computation.1 | async-start | bytes 4980736
  165.8 3.7 copy-start.1
  362.3 10.0 %copy-start.2 = (f32[7680]{0:T(1024)S(1)}, f32[7680]{0:T(1024)}, u32[]{:S(2)}) copy-start(f32[7680]{0:T(1024)} %reshape.300) | copy-start | bytes 92164
  362.3 14.6 %copy-start.3 = (f32[7680]{0:T(1024)S(1)}, f32[7680]{0:T(1024)}, u32[]{:S(2)}) copy-start(f32[7680]{0:T(1024)} %reshape.303) | copy-start | bytes 92164
  363.6 17.1 %copy-start.4 = (f32[7680]{0:T(1024)S(1)}, f32[7680]{0:T(1024)}, u32[]{:S(2)}) copy-start(f32[7680]{0:T(1024)} %reshape.306) | copy-start | bytes 92164
Sparse Core Ops, SparseCore 0:
  14.0 133.2 all-reduce.12
  387.2 135.4 all-reduce.14
